TPU v7x, 32 devices: a whole 2x2x4 slice. The times are simulated.
32 devices in a mesh: grp: 4 (over x, core), wav: 8 (over z, y).
Axes of the slice: x: 2, y: 2, z: 4, core: 2. Of those that a mesh axis runs over, the one named last changes fastest.
Arguments:
- spectra: float32 [3, 8, 16, 2, 2560], P(None, 'grp', 'wav'), may hold values from -6 to 6
- legendre: float32 [16, 2560, 32], P('wav'), may hold values from -0.03125 to 0.03125
- wave_number: int32 [16], replicated, may hold values from 0 to 2559, as said below
- cycle_points: int32 [32], replicated, may hold values from 20 to 10256, as said below
- cycle_owner: int32 [64], replicated, may hold values from 0 to 63, each once
Outputs:
- grid_columns: float32 [64, 3, 8, 11264], P('grp', None, None, 'wav')
Inputs may be any that keep to these rules, and one draw needn't show every extreme that they name: `wave_number`: all distinct; entries 2 i and 2 i + 1 sum to 2559. `cycle_points`: each is 20 + 4 k for a whole k, rising with the latitude index; 20 and 10256 both occur. `cycle_owner`: A permutation of the cycles: 0 to 31 northern, 32 + i the southern mirror of latitude i.
All inputs are finite; a program needn't handle non-finite values.
Results may differ from a plain program's by a relative error of at most 0.0003.
Values sent between devices are 32-bit elements; how exact they have to be, the bound alone decides.
A program may use at most 128 MiB of HBM per device.

v0:
```python
import jax
import jax.numpy as jnp
from jax import lax
from jax.sharding import PartitionSpec as P

RMAX = 10256
TWO_PI = 6.283185307179586
HIGHEST = lax.Precision.HIGHEST


def synthesis(coeffs, wave_list, lengths, points_count):
    points = jnp.arange(points_count, dtype=jnp.int32)
    weight = jnp.where(wave_list == 0, 1.0, 2.0).astype(jnp.float32)
    wave_total = wave_list.shape[0]

    def one_cycle(cycle_args):
        cycle_block, cycle_length = cycle_args
        phases = wave_list[:, None] * points[None, :] % cycle_length
        angles = phases.astype(jnp.float32) * (TWO_PI / cycle_length.astype(jnp.float32))
        cosine = weight[:, None] * jnp.cos(angles)
        sine_part = -weight[:, None] * jnp.sin(angles)
        fourier_basis = jnp.stack([cosine, sine_part], axis=1).reshape(2 * wave_total, points_count)
        flattened = cycle_block.reshape(-1, 2 * wave_total)
        values = jnp.dot(
            flattened, fourier_basis, precision=HIGHEST, preferred_element_type=jnp.float32
        )
        values = jnp.where(points[None, :] < cycle_length, values, 0.0)
        return values.reshape(cycle_block.shape[:-1] + (points_count,))

    return lax.map(one_cycle, (coeffs, lengths))


def body(spectra, legendre, wave_number, cycle_points, cycle_owner):
    column = lax.axis_index("wav")
    wav_size = lax.axis_size("wav")
    wave_local = legendre.shape[0]
    degree_rows = legendre.shape[1]
    my_waves = lax.dynamic_slice_in_dim(wave_number, column * wave_local, wave_local)
    offsets = jnp.arange(degree_rows, dtype=jnp.int32)
    inside = my_waves[:, None] + offsets[None, :] < degree_rows
    masked = jnp.where(inside[None, None, :, None, :], spectra, 0.0)
    parity_signs = jnp.where(offsets % 2 == 0, 1.0, -1.0).astype(jnp.float32)
    mirrored = jnp.concatenate([legendre, legendre * parity_signs[None, :, None]], axis=2)
    fourier = jnp.einsum("flmck,mki->iflmc", masked, mirrored, precision=HIGHEST)
    placed = jnp.take(fourier, cycle_owner, axis=0)
    cycle_total = placed.shape[0]
    rows_first = placed.reshape(cycle_total, 3, placed.shape[2], 2 * wave_local)
    cycle_lengths = jnp.concatenate([cycle_points, cycle_points])[cycle_owner]
    segment = (RMAX + 128 * wav_size - 1) // (128 * wav_size) * 128
    owned_cycles = cycle_total // wav_size
    my_lengths = lax.dynamic_slice_in_dim(cycle_lengths, column * owned_cycles, owned_cycles)
    grid_rows = synthesis(
        lax.all_to_all(rows_first, "wav", split_axis=0, concat_axis=3, tiled=True),
        wave_number,
        my_lengths,
        segment * wav_size,
    )
    return lax.all_to_all(
        lax.all_to_all(grid_rows, "wav", split_axis=3, concat_axis=0, tiled=True),
        "grp",
        split_axis=0,
        concat_axis=2,
        tiled=True,
    )


def solution(mesh):
    in_specs = (P(None, "grp", "wav", None, None), P("wav", None, None), P(), P(), P())
    out_specs = P("grp", None, None, "wav")
    return jax.shard_map(body, mesh=mesh, in_specs=in_specs, out_specs=out_specs, check_vma=False)
```

profile of v0, /device:TPU:0, one launch (start us, length us, event | category | flops | bytes accessed | tf_op | source)
XLA Modules:
  0.0 470.3 jit_solution(11848832850669531149)
XLA Ops:
  0.0 0.7 compare_and_fusion
  0.7 0.7 compare_select_fusion
  1.3 0.7 dynamic_slice.17
  2.2 1.1 broadcast_select_fusion
  3.3 1.1 broadcast_multiply_fusion
  4.4 2.4 fusion.16
  7.1 0.8 gather_fusion.1
  8.3 0.9 reshape.234
  9.2 7.3 %all-to-all-start = ((f32[8,1,192]{2,1,0:T(1,128)}), f32[8,1,192]{2,1,0:T(1,128)S(1)}, u32[]{:S(2)}, u32[]{:S(2)}) async-start(f32[8,1,192]{2,1,0:T(1,128)} %reshape.234), calls=%async_computation | async-start | bytes 16384 | tf_op jit(solution)/shard_map/all_to_all | solution.py:53
  16.5 0.8 gather_fusion
  17.4 5.6 %all-to-all-done = f32[8,1,192]{2,1,0:T(1,128)S(1)} async-done(((f32[8,1,192]{2,1,0:T(1,128)}), f32[8,1,192]{2,1,0:T(1,128)S(1)}, u32[]{:S(2)}, u32[]{:S(2)}) %all-to-all-start) | async-done | bytes 6176 | tf_op jit(solution)/shard_map/all_to_all | solution.py:53
  23.5 0.7 reduce
  25.0 134.5 %while.13 = (s32[]{:T(128)}, f32[8,3,2,11264]{3,2,1,0:T(2,128)}, s32[8]{0:T(128)S(1)}, f32[8,3,2,32]{3,2,1,0:T(2,128)S(1)}, f32[16]{0:T(128)S(1)}, /*index=5*/s3...) while((s32[]{:T(128)}, f32[8,3,2,11264]{3,2,1,0:T(2,128)}, ...), condition=%wide.region_1.2_spmd.clone.clone, body=%wide.region_0.1_spmd.clone.clone.sunk | while | flops 28554248 | bytes 12912769 | solution.py:30
  28.4 9.6 %fusion.31 = (f32[16,1,11264]{2,0,1:T(8,128)S(1)}, f32[16,1,11264]{2,0,1:T(8,128)S(1)}) fusion(f32[]{:T(128)S(6)} %div.7, s32[]{:T(128)S(6)} %select_n.118, s32[16]{0:T(128)S(1)} %get-tuple-element.247, f32[16]{0:T(128)S(1)} %get-tuple-element.246, pred[]{:T(512)S(6)} %lt.122, f32[16]{0:T(128)S(1)} %bitcast.47), kind=kLoop, calls=%fused_computation.14.clone.1 | loop fusion | flops 2162688 | bytes 1441993 | tf_op jit(solution)/shard_map/while/body/eval_jaxpr/mul | solution.py:20
  38.1 1.1 copy.85
  39.2 1.0 reshape.241
  40.2 0.8 convolution_select_fusion.2
  41.2 0.7 constant_dynamic-update-slice_fusion.2
  45.2 9.6 %fusion.31 = (f32[16,1,11264]{2,0,1:T(8,128)S(1)}, f32[16,1,11264]{2,0,1:T(8,128)S(1)}) fusion(f32[]{:T(128)S(6)} %div.7, s32[]{:T(128)S(6)} %select_n.118, s32[16]{0:T(128)S(1)} %get-tuple-element.247, f32[16]{0:T(128)S(1)} %get-tuple-element.246, pred[]{:T(512)S(6)} %lt.122, f32[16]{0:T(128)S(1)} %bitcast.47), kind=kLoop, calls=%fused_computation.14.clone.1 | loop fusion | flops 2162688 | bytes 1441993 | tf_op jit(solution)/shard_map/while/body/eval_jaxpr/mul | solution.py:20
  54.8 1.1 copy.85
  56.0 1.0 reshape.241
  57.0 0.8 convolution_select_fusion.2
  57.9 0.7 constant_dynamic-update-slice_fusion.2
  61.2 0.6 iota_compare_fusion.2
  61.9 9.6 %fusion.31 = (f32[16,1,11264]{2,0,1:T(8,128)S(1)}, f32[16,1,11264]{2,0,1:T(8,128)S(1)}) fusion(f32[]{:T(128)S(6)} %div.7, s32[]{:T(128)S(6)} %select_n.118, s32[16]{0:T(128)S(1)} %get-tuple-element.247, f32[16]{0:T(128)S(1)} %get-tuple-element.246, pred[]{:T(512)S(6)} %lt.122, f32[16]{0:T(128)S(1)} %bitcast.47), kind=kLoop, calls=%fused_computation.14.clone.1 | loop fusion | flops 2162688 | bytes 1441993 | tf_op jit(solution)/shard_map/while/body/eval_jaxpr/mul | solution.py:20
  71.6 1.1 copy.85
  72.7 1.0 reshape.241
  73.7 0.8 convolution_select_fusion.2
  74.7 0.7 constant_dynamic-update-slice_fusion.2
  78.6 9.6 %fusion.31 = (f32[16,1,11264]{2,0,1:T(8,128)S(1)}, f32[16,1,11264]{2,0,1:T(8,128)S(1)}) fusion(f32[]{:T(128)S(6)} %div.7, s32[]{:T(128)S(6)} %select_n.118, s32[16]{0:T(128)S(1)} %get-tuple-element.247, f32[16]{0:T(128)S(1)} %get-tuple-element.246, pred[]{:T(512)S(6)} %lt.122, f32[16]{0:T(128)S(1)} %bitcast.47), kind=kLoop, calls=%fused_computation.14.clone.1 | loop fusion | flops 2162688 | bytes 1441993 | tf_op jit(solution)/shard_map/while/body/eval_jaxpr/mul | solution.py:20
  88.3 1.1 copy.85
  89.4 1.0 reshape.241
  90.4 0.8 convolution_select_fusion.2
  91.4 0.7 constant_dynamic-update-slice_fusion.2
  95.4 9.6 %fusion.31 = (f32[16,1,11264]{2,0,1:T(8,128)S(1)}, f32[16,1,11264]{2,0,1:T(8,128)S(1)}) fusion(f32[]{:T(128)S(6)} %div.7, s32[]{:T(128)S(6)} %select_n.118, s32[16]{0:T(128)S(1)} %get-tuple-element.247, f32[16]{0:T(128)S(1)} %get-tuple-element.246, pred[]{:T(512)S(6)} %lt.122, f32[16]{0:T(128)S(1)} %bitcast.47), kind=kLoop, calls=%fused_computation.14.clone.1 | loop fusion | flops 2162688 | bytes 1441993 | tf_op jit(solution)/shard_map/while/body/eval_jaxpr/mul | solution.py:20
  105.1 1.1 copy.85
  106.2 1.0 reshape.241
  107.2 0.8 convolution_select_fusion.2
  108.1 0.7 constant_dynamic-update-slice_fusion.2
  111.5 0.6 iota_compare_fusion.2
  112.1 9.6 %fusion.31 = (f32[16,1,11264]{2,0,1:T(8,128)S(1)}, f32[16,1,11264]{2,0,1:T(8,128)S(1)}) fusion(f32[]{:T(128)S(6)} %div.7, s32[]{:T(128)S(6)} %select_n.118, s32[16]{0:T(128)S(1)} %get-tuple-element.247, f32[16]{0:T(128)S(1)} %get-tuple-element.246, pred[]{:T(512)S(6)} %lt.122, f32[16]{0:T(128)S(1)} %bitcast.47), kind=kLoop, calls=%fused_computation.14.clone.1 | loop fusion | flops 2162688 | bytes 1441993 | tf_op jit(solution)/shard_map/while/body/eval_jaxpr/mul | solution.py:20
  121.8 1.1 copy.85
  122.9 1.0 reshape.241
  123.9 0.8 convolution_select_fusion.2
  124.9 0.7 constant_dynamic-update-slice_fusion.2
  128.9 9.6 %fusion.31 = (f32[16,1,11264]{2,0,1:T(8,128)S(1)}, f32[16,1,11264]{2,0,1:T(8,128)S(1)}) fusion(f32[]{:T(128)S(6)} %div.7, s32[]{:T(128)S(6)} %select_n.118, s32[16]{0:T(128)S(1)} %get-tuple-element.247, f32[16]{0:T(128)S(1)} %get-tuple-element.246, pred[]{:T(512)S(6)} %lt.122, f32[16]{0:T(128)S(1)} %bitcast.47), kind=kLoop, calls=%fused_computation.14.clone.1 | loop fusion | flops 2162688 | bytes 1441993 | tf_op jit(solution)/shard_map/while/body/eval_jaxpr/mul | solution.py:20
  138.5 1.1 copy.85
  139.7 1.0 reshape.241
  140.7 0.8 convolution_select_fusion.2
  141.6 0.7 constant_dynamic-update-slice_fusion.2
  145.6 9.6 %fusion.31 = (f32[16,1,11264]{2,0,1:T(8,128)S(1)}, f32[16,1,11264]{2,0,1:T(8,128)S(1)}) fusion(f32[]{:T(128)S(6)} %div.7, s32[]{:T(128)S(6)} %select_n.118, s32[16]{0:T(128)S(1)} %get-tuple-element.247, f32[16]{0:T(128)S(1)} %get-tuple-element.246, pred[]{:T(512)S(6)} %lt.122, f32[16]{0:T(128)S(1)} %bitcast.47), kind=kLoop, calls=%fused_computation.14.clone.1 | loop fusion | flops 2162688 | bytes 1441993 | tf_op jit(solution)/shard_map/while/body/eval_jaxpr/mul | solution.py:20
  155.3 1.1 copy.85
  156.4 1.0 reshape.241
  157.4 0.8 convolution_select_fusion.2
  158.4 0.7 constant_dynamic-update-slice_fusion.2
  159.5 35.7 %copy.71 = f32[8,3,2,11264]{0,2,1,3:T(2,128)} copy(f32[8,3,2,11264]{3,2,1,0:T(2,128)} %get-tuple-element.78) | data formatting | bytes 4325376 | tf_op jit(solution)/shard_map/while | solution.py:30
  195.2 73.8 %reshape.236 = f32[8,1,67584]{2,1,0:T(1,128)S(1)} reshape(f32[11264,3,2,8]{3,2,1,0:T(2,128)} %bitcast.38) | data formatting | bytes 4325376
  269.0 52.3 %all_to_all.54 = f32[8,1,67584]{2,1,0:T(1,128)} all-to-all(f32[8,1,67584]{2,1,0:T(1,128)S(1)} %reshape.236), channel_id=1, replica_groups=mesh['grp'=4,'wav'=8] {'wav'}, dimensions={0} | all-to-all | bytes 4325376 | tf_op jit(solution)/shard_map/all_to_all | solution.py:59
  321.3 7.4 %reduce.1 = f32[8,67584]{1,0:T(8,128)S(1)} reduce(f32[8,1,67584]{2,1,0:T(1,128)} %all_to_all.54, f32[]{:T(128)} %broadcast.245), dimensions={1}, to_apply=%all_to_all.43.reduce_sub_computation | reduce | bytes 4325380 | tf_op jit(solution)/shard_map/all_to_all | solution.py:59
  328.7 67.0 %reshape.237 = f32[11264,3,2,8]{3,2,1,0:T(2,128)} reshape(f32[8,67584]{1,0:T(8,128)S(1)} %reduce.1) | data formatting | bytes 4325376
  395.6 41.3 %copy.81 = f32[8,3,2,8,1408]{4,0,3,2,1:T(8,128)S(1)} copy(f32[8,3,2,8,1408]{0,2,1,4,3:T(2,128)} %bitcast.39) | data formatting | bytes 4325376 | tf_op jit(solution)/shard_map/all_to_all | solution.py:59
  437.0 1.7 copy.74
  438.7 29.0 %all_to_all.55 = f32[64,3,2,1408]{3,2,1,0:T(2,128)S(1)} all-to-all(f32[64,3,2,1408]{3,2,1,0:T(2,128)S(1)} %copy.74), channel_id=1, replica_groups=mesh['grp'=4,'wav'=8] {'grp'}, dimensions={0} | all-to-all | bytes 4325376 | tf_op jit(solution)/shard_map/all_to_all | solution.py:58
  468.0 2.0 copy.77
  (68 shorter events, 13.5 us)
Async XLA Ops:
  3.2 13.2 %copy-start = (s32[16]{0:T(128)S(1)}, s32[16]{0:T(128)}, u32[]{:S(2)}) copy-start(s32[16]{0:T(128)} %param.9) | copy-start | bytes 196
  3.2 13.2 %copy-start.1 = (s32[32]{0:T(128)S(1)}, s32[32]{0:T(128)}, u32[]{:S(2)}) copy-start(s32[32]{0:T(128)} %param.10) | copy-start | bytes 388
  9.2 13.8 %all-to-all-start = ((f32[8,1,192]{2,1,0:T(1,128)}), f32[8,1,192]{2,1,0:T(1,128)S(1)}, u32[]{:S(2)}, u32[]{:S(2)}) async-start(f32[8,1,192]{2,1,0:T(1,128)} %reshape.234), calls=%async_computation | async-start | bytes 16384 | tf_op jit(solution)/shard_map/all_to_all | solution.py:53
where the time goes:
time: 478 us; the launch traced here: 470 us
  local copies, waits for them, and re-layouts  256 us (54%)
  other arithmetic  94.3 us (20%)
  blocking collectives  81.2 us (17%)
  loops' own time  16.6 us (3%)
  matrix products  8.78 us (2%)
  starting transfers between devices  7.28 us (2%)
  waiting for transfers between devices  5.56 us (1%)
    unnamed x9, local copies, waits for them, and re-layouts  142 us
    mul x8, other arithmetic, one_cycle(): cosine = weight[:, None] * jnp.cos(angles)  76.7 us
    all_to_all x1, blocking collectives, body(): lax.all_to_all(grid_rows, 'wav', split_axis=3, concat_axis=0, tiled=True)  52.3 us
    all_to_all x2, local copies, waits for them, and re-layouts, body(): lax.all_to_all(grid_rows, 'wav', split_axis=3, concat_axis=0, tiled=True)  43 us
    while x1, local copies, waits for them, and re-layouts, synthesis(): return lax.map(one_cycle, (coeffs, lengths))  35.7 us
    all_to_all x1, blocking collectives, body(): lax.all_to_all(lax.all_to_all(grid_rows, 'wav', split_axis=3, concat_axis...  29 us
    another operation x1, loops' own time, synthesis(): return lax.map(one_cycle, (coeffs, lengths))  16.6 us
  transfers between devices with their start and end apart: 1, of which 1 were waited for; matrix products, arithmetic and copies ran while one was open for 0% of the time, Pallas kernels for 0%

commit v1 on v0

--- a/solution.py
+++ b/solution.py
@@ -6,6 +6,18 @@
 RMAX = 10256
 TWO_PI = 6.283185307179586
 HIGHEST = lax.Precision.HIGHEST
+
+
+def sent_to_each(shard, axis, split, join):
+    ways, here = (lax.axis_size(axis), lax.axis_index(axis))
+    width = shard.shape[split] // ways
+    turned = jnp.roll(shard, -here * width, axis=split)
+    got = [lax.slice_in_dim(turned, 0, width, axis=split)]
+    for far in range(1, ways):
+        sent = lax.slice_in_dim(turned, far * width, (far + 1) * width, axis=split)
+        got.append(lax.ppermute(sent, axis, [(d, (d + far) % ways) for d in range(ways)]))
+    line = jnp.concatenate(got[::-1], axis=join)
+    return jnp.roll(line, (here + 1) * got[0].shape[join], axis=join)
 
 
 def synthesis(coeffs, wave_list, lengths, points_count):
@@ -50,10 +62,7 @@
     owned_cycles = cycle_total // wav_size
     my_lengths = lax.dynamic_slice_in_dim(cycle_lengths, column * owned_cycles, owned_cycles)
     grid_rows = synthesis(
-        lax.all_to_all(rows_first, "wav", split_axis=0, concat_axis=3, tiled=True),
-        wave_number,
-        my_lengths,
-        segment * wav_size,
+        sent_to_each(rows_first, "wav", 0, 3), wave_number, my_lengths, segment * wav_size
     )
     return lax.all_to_all(
         lax.all_to_all(grid_rows, "wav", split_axis=3, concat_axis=0, tiled=True),

time: 478 us -> 478 us (level)
  starting transfers between devices: 7.28 us -> 12.5 us
    ppermute x0 -> x7, starting transfers between devices: none -> 12.5 us  [sent_to_each(): lax.ppermute(sent, axis, [(d, (d + far) % ways) for d in range(ways)])]
    all_to_all x1 -> x0, starting transfers between devices: 7.28 us -> none  [body(): lax.all_to_all(rows_first, 'wav', split_axis=0, concat_axis=3, tiled=True)]
    all_to_all x1 -> x0, waiting for transfers between devices: 5.56 us -> none  [body(): lax.all_to_all(rows_first, 'wav', split_axis=0, concat_axis=3, tiled=True)]
    unnamed x9 -> x8, local copies, waits for them, and re-layouts: 142 us -> 141 us
    all_to_all x2 -> x3, local copies, waits for them, and re-layouts: 43 us -> 43.5 us  [body(): lax.all_to_all(grid_rows, 'wav', split_axis=3, concat_axis=0, tiled=True)]
  transfers between devices with their start and end apart: 1 -> 7, of which waited for: 1 -> 3; matrix products, arithmetic and copies ran while one was open for 0% -> 0% of each run, Pallas kernels for 0% -> 0%
where the time goes in v1:
time: 478 us; the launch traced here: 470 us
  local copies, waits for them, and re-layouts  255 us (53%)
  other arithmetic  92.4 us (19%)
  blocking collectives  79.9 us (17%)
  loops' own time  16.6 us (3%)
  starting transfers between devices  12.5 us (3%)
  matrix products  8.78 us (2%)
    unnamed x8, local copies, waits for them, and re-layouts  141 us
    mul x8, other arithmetic, one_cycle(): cosine = weight[:, None] * jnp.cos(angles)  76.6 us
    all_to_all x1, blocking collectives, body(): lax.all_to_all(grid_rows, 'wav', split_axis=3, concat_axis=0, tiled=True)  50.9 us
    all_to_all x3, local copies, waits for them, and re-layouts, body(): lax.all_to_all(grid_rows, 'wav', split_axis=3, concat_axis=0, tiled=True)  43.5 us
    while x1, local copies, waits for them, and re-layouts, synthesis(): return lax.map(one_cycle, (coeffs, lengths))  35.7 us
    all_to_all x1, blocking collectives, body(): lax.all_to_all(lax.all_to_all(grid_rows, 'wav', split_axis=3, concat_axis...  29 us
    another operation x1, loops' own time, synthesis(): return lax.map(one_cycle, (coeffs, lengths))  16.6 us
    ppermute x7, starting transfers between devices, sent_to_each(): lax.ppermute(sent, axis, [(d, (d + far) % ways) for d in range(ways)])  12.5 us
  transfers between devices with their start and end apart: 7, of which 3 were waited for; matrix products, arithmetic and copies ran while one was open for 0% of the time, Pallas kernels for 0%

profile of v1, /device:TPU:0, one launch (start us, length us, event | category | flops | bytes accessed | tf_op | source)
XLA Modules:
  0.0 469.9 jit_solution(13260142557726816903)
XLA Ops:
  0.0 0.7 dynamic_slice.25
  0.9 1.1 broadcast_select_fusion
  1.9 1.1 broadcast_multiply_fusion
  3.1 2.4 fusion.16
  5.9 0.8 gather_fusion.1
  7.1 6.1 %collective-permute-start = (f32[8,3,2,4]{0,3,2,1:T(4,128)S(1)}, f32[8,3,2,4]{0,3,2,1:T(4,128)S(1)}, u32[]{:S(2)}, u32[]{:S(2)}) collective-permute-start(f32[8,3,2,4]{0,3,2,1:T(4,128)S(1)} %get-tuple-element.180), channel_id=1, source_target_pairs={{0,7},{1,0},{2,1},{3,2},{4,3},{5,4},{6,5},{7,6},{8,15},{9,8},{10,9... | collective-permute-start | bytes 2312 | tf_op jit(solution)/shard_map/ppermute | solution.py:18
  13.6 3.0 collective-permute-start.3
  16.7 1.9 collective-permute-start.5
  18.6 1.1 collective-permute-start.6
  19.7 0.8 gather_fusion
  21.0 1.1 collective-permute-done.4
  22.2 1.0 collective-permute-done.5
  23.3 1.7 collective-permute-done.6
  25.3 134.4 %while.13 = (s32[]{:T(128)}, f32[8,3,2,11264]{3,2,1,0:T(2,128)}, s32[8]{0:T(128)S(1)}, f32[8,3,2,32]{3,0,2,1:T(8,128)S(1)}, f32[16]{0:T(128)S(1)}, /*index=5*/s3...) while((s32[]{:T(128)}, f32[8,3,2,11264]{3,2,1,0:T(2,128)}, ...), condition=%wide.region_1.2_spmd.clone.clone, body=%wide.region_0.1_spmd.clone.clone.sunk | while | flops 28554248 | bytes 12913269 | solution.py:42
  28.1 9.6 %fusion.32 = (f32[16,1,11264]{2,0,1:T(8,128)S(1)}, f32[16,1,11264]{2,0,1:T(8,128)S(1)}) fusion(f32[]{:T(128)S(6)} %div.7, s32[]{:T(128)S(6)} %select_n.144, s32[16]{0:T(128)S(1)} %get-tuple-element.257, f32[16]{0:T(128)S(1)} %get-tuple-element.256, pred[]{:T(512)S(6)} %lt.148, f32[16]{0:T(128)S(1)} %bitcast.45), kind=kLoop, calls=%fused_computation.14.clone.1 | loop fusion | flops 2162688 | bytes 1441993 | tf_op jit(solution)/shard_map/while/body/eval_jaxpr/mul | solution.py:32
  37.8 1.1 copy.135
  38.9 1.0 reshape.239
  39.9 0.6 iota_compare_fusion.2
  40.6 0.8 convolution_select_fusion.2
  41.5 0.7 constant_dynamic-update-slice_fusion.2
  44.8 9.6 %fusion.32 = (f32[16,1,11264]{2,0,1:T(8,128)S(1)}, f32[16,1,11264]{2,0,1:T(8,128)S(1)}) fusion(f32[]{:T(128)S(6)} %div.7, s32[]{:T(128)S(6)} %select_n.144, s32[16]{0:T(128)S(1)} %get-tuple-element.257, f32[16]{0:T(128)S(1)} %get-tuple-element.256, pred[]{:T(512)S(6)} %lt.148, f32[16]{0:T(128)S(1)} %bitcast.45), kind=kLoop, calls=%fused_computation.14.clone.1 | loop fusion | flops 2162688 | bytes 1441993 | tf_op jit(solution)/shard_map/while/body/eval_jaxpr/mul | solution.py:32
  54.5 1.1 copy.135
  55.6 1.0 reshape.239
  57.3 0.8 convolution_select_fusion.2
  58.3 0.7 constant_dynamic-update-slice_fusion.2
  61.5 9.6 %fusion.32 = (f32[16,1,11264]{2,0,1:T(8,128)S(1)}, f32[16,1,11264]{2,0,1:T(8,128)S(1)}) fusion(f32[]{:T(128)S(6)} %div.7, s32[]{:T(128)S(6)} %select_n.144, s32[16]{0:T(128)S(1)} %get-tuple-element.257, f32[16]{0:T(128)S(1)} %get-tuple-element.256, pred[]{:T(512)S(6)} %lt.148, f32[16]{0:T(128)S(1)} %bitcast.45), kind=kLoop, calls=%fused_computation.14.clone.1 | loop fusion | flops 2162688 | bytes 1441993 | tf_op jit(solution)/shard_map/while/body/eval_jaxpr/mul | solution.py:32
  71.2 1.1 copy.135
  72.3 1.0 reshape.239
  74.0 0.8 convolution_select_fusion.2
  75.0 0.7 constant_dynamic-update-slice_fusion.2
  78.3 9.6 %fusion.32 = (f32[16,1,11264]{2,0,1:T(8,128)S(1)}, f32[16,1,11264]{2,0,1:T(8,128)S(1)}) fusion(f32[]{:T(128)S(6)} %div.7, s32[]{:T(128)S(6)} %select_n.144, s32[16]{0:T(128)S(1)} %get-tuple-element.257, f32[16]{0:T(128)S(1)} %get-tuple-element.256, pred[]{:T(512)S(6)} %lt.148, f32[16]{0:T(128)S(1)} %bitcast.45), kind=kLoop, calls=%fused_computation.14.clone.1 | loop fusion | flops 2162688 | bytes 1441993 | tf_op jit(solution)/shard_map/while/body/eval_jaxpr/mul | solution.py:32
  88.0 1.1 copy.135
  89.1 1.0 reshape.239
  90.8 0.8 convolution_select_fusion.2
  91.7 0.7 constant_dynamic-update-slice_fusion.2
  95.0 9.6 %fusion.32 = (f32[16,1,11264]{2,0,1:T(8,128)S(1)}, f32[16,1,11264]{2,0,1:T(8,128)S(1)}) fusion(f32[]{:T(128)S(6)} %div.7, s32[]{:T(128)S(6)} %select_n.144, s32[16]{0:T(128)S(1)} %get-tuple-element.257, f32[16]{0:T(128)S(1)} %get-tuple-element.256, pred[]{:T(512)S(6)} %lt.148, f32[16]{0:T(128)S(1)} %bitcast.45), kind=kLoop, calls=%fused_computation.14.clone.1 | loop fusion | flops 2162688 | bytes 1441993 | tf_op jit(solution)/shard_map/while/body/eval_jaxpr/mul | solution.py:32
  104.7 1.1 copy.135
  105.8 1.0 reshape.239
  107.5 0.8 convolution_select_fusion.2
  108.5 0.7 constant_dynamic-update-slice_fusion.2
  111.7 9.6 %fusion.32 = (f32[16,1,11264]{2,0,1:T(8,128)S(1)}, f32[16,1,11264]{2,0,1:T(8,128)S(1)}) fusion(f32[]{:T(128)S(6)} %div.7, s32[]{:T(128)S(6)} %select_n.144, s32[16]{0:T(128)S(1)} %get-tuple-element.257, f32[16]{0:T(128)S(1)} %get-tuple-element.256, pred[]{:T(512)S(6)} %lt.148, f32[16]{0:T(128)S(1)} %bitcast.45), kind=kLoop, calls=%fused_computation.14.clone.1 | loop fusion | flops 2162688 | bytes 1441993 | tf_op jit(solution)/shard_map/while/body/eval_jaxpr/mul | solution.py:32
  121.4 1.1 copy.135
  122.6 1.0 reshape.239
  124.2 0.8 convolution_select_fusion.2
  125.2 0.7 constant_dynamic-update-slice_fusion.2
  128.5 9.6 %fusion.32 = (f32[16,1,11264]{2,0,1:T(8,128)S(1)}, f32[16,1,11264]{2,0,1:T(8,128)S(1)}) fusion(f32[]{:T(128)S(6)} %div.7, s32[]{:T(128)S(6)} %select_n.144, s32[16]{0:T(128)S(1)} %get-tuple-element.257, f32[16]{0:T(128)S(1)} %get-tuple-element.256, pred[]{:T(512)S(6)} %lt.148, f32[16]{0:T(128)S(1)} %bitcast.45), kind=kLoop, calls=%fused_computation.14.clone.1 | loop fusion | flops 2162688 | bytes 1441993 | tf_op jit(solution)/shard_map/while/body/eval_jaxpr/mul | solution.py:32
  138.2 1.1 copy.135
  139.3 1.0 reshape.239
  141.0 0.8 convolution_select_fusion.2
  141.9 0.7 constant_dynamic-update-slice_fusion.2
  145.2 9.6 %fusion.32 = (f32[16,1,11264]{2,0,1:T(8,128)S(1)}, f32[16,1,11264]{2,0,1:T(8,128)S(1)}) fusion(f32[]{:T(128)S(6)} %div.7, s32[]{:T(128)S(6)} %select_n.144, s32[16]{0:T(128)S(1)} %get-tuple-element.257, f32[16]{0:T(128)S(1)} %get-tuple-element.256, pred[]{:T(512)S(6)} %lt.148, f32[16]{0:T(128)S(1)} %bitcast.45), kind=kLoop, calls=%fused_computation.14.clone.1 | loop fusion | flops 2162688 | bytes 1441993 | tf_op jit(solution)/shard_map/while/body/eval_jaxpr/mul | solution.py:32
  154.9 1.1 copy.135
  156.0 1.0 reshape.239
  157.7 0.8 convolution_select_fusion.2
  158.7 0.7 constant_dynamic-update-slice_fusion.2
  159.8 35.7 %copy.121 = f32[8,3,2,11264]{0,2,1,3:T(2,128)} copy(f32[8,3,2,11264]{3,2,1,0:T(2,128)} %get-tuple-element.78) | data formatting | bytes 4325376 | tf_op jit(solution)/shard_map/while | solution.py:42
  195.5 73.8 %reshape.234 = f32[8,1,67584]{2,1,0:T(1,128)S(1)} reshape(f32[11264,3,2,8]{3,2,1,0:T(2,128)} %bitcast.38) | data formatting | bytes 4325376
  269.3 50.9 %all_to_all.36 = f32[8,1,67584]{2,1,0:T(1,128)} all-to-all(f32[8,1,67584]{2,1,0:T(1,128)S(1)} %reshape.234), channel_id=1, replica_groups=mesh['grp'=4,'wav'=8] {'wav'}, dimensions={0} | all-to-all | bytes 4325376 | tf_op jit(solution)/shard_map/all_to_all | solution.py:68
  320.8 7.4 %reduce = f32[8,67584]{1,0:T(8,128)S(1)} reduce(f32[8,1,67584]{2,1,0:T(1,128)} %all_to_all.36, f32[]{:T(128)} %broadcast.247), dimensions={1}, to_apply=%all_to_all.26.reduce_sub_computation | reduce | bytes 4325380 | tf_op jit(solution)/shard_map/all_to_all | solution.py:68
  328.2 67.1 %reshape.235 = f32[11264,3,2,8]{3,2,1,0:T(2,128)} reshape(f32[8,67584]{1,0:T(8,128)S(1)} %reduce) | data formatting | bytes 4325376
  395.3 41.3 %copy.130 = f32[8,3,2,8,1408]{4,0,3,2,1:T(8,128)S(1)} copy(f32[8,3,2,8,1408]{0,2,1,4,3:T(2,128)} %bitcast.39) | data formatting | bytes 4325376 | tf_op jit(solution)/shard_map/all_to_all | solution.py:68
  436.6 1.7 copy.124
  438.3 29.0 %all_to_all.37 = f32[64,3,2,1408]{3,2,1,0:T(2,128)S(1)} all-to-all(f32[64,3,2,1408]{3,2,1,0:T(2,128)S(1)} %copy.124), channel_id=1, replica_groups=mesh['grp'=4,'wav'=8] {'grp'}, dimensions={0} | all-to-all | bytes 4325376 | tf_op jit(solution)/shard_map/all_to_all | solution.py:67
  467.7 2.0 copy.127
  (86 shorter events, 14.9 us)
Async XLA Ops:
  0.0 5.8 %copy-start.1 = (s32[64]{0:T(128)S(1)}, s32[64]{0:T(128)}, u32[]{:S(2)}) copy-start(s32[64]{0:T(128)} %param.11) | copy-start | bytes 772
  0.0 5.8 %copy-start.2 = (s32[32]{0:T(128)S(1)}, s32[32]{0:T(128)}, u32[]{:S(2)}) copy-start(s32[32]{0:T(128)} %param.10) | copy-start | bytes 388
  1.9 14.7 %copy-start = (s32[16]{0:T(128)S(1)}, s32[16]{0:T(128)}, u32[]{:S(2)}) copy-start(s32[16]{0:T(128)} %param.9) | copy-start | bytes 196
  7.1 9.6 %collective-permute-start = (f32[8,3,2,4]{0,3,2,1:T(4,128)S(1)}, f32[8,3,2,4]{0,3,2,1:T(4,128)S(1)}, u32[]{:S(2)}, u32[]{:S(2)}) collective-permute-start(f32[8,3,2,4]{0,3,2,1:T(4,128)S(1)} %get-tuple-element.180), channel_id=1, source_target_pairs={{0,7},{1,0},{2,1},{3,2},{4,3},{5,4},{6,5},{7,6},{8,15},{9,8},{10,9... | collective-permute-start | bytes 2312 | tf_op jit(solution)/shard_map/ppermute | solution.py:18
  13.1 5.4 %collective-permute-start.1 = (f32[8,3,2,4]{0,3,2,1:T(4,128)S(1)}, f32[8,3,2,4]{0,3,2,1:T(4,128)S(1)}, u32[]{:S(2)}, u32[]{:S(2)}) collective-permute-start(f32[8,3,2,4]{0,3,2,1:T(4,128)S(1)} %get-tuple-element.179), channel_id=1, source_target_pairs={{0,6},{1,7},{2,0},{3,1},{4,2},{5,3},{6,4},{7,5},{8,14},{9,15},{10,... | collective-permute-start | bytes 2312 | tf_op jit(solution)/shard_map/ppermute | solution.py:18
  13.6 7.2 %collective-permute-start.2 = (f32[8,3,2,4]{0,3,2,1:T(4,128)S(1)}, f32[8,3,2,4]{0,3,2,1:T(4,128)S(1)}, u32[]{:S(2)}, u32[]{:S(2)}) collective-permute-start(f32[8,3,2,4]{0,3,2,1:T(4,128)S(1)} %get-tuple-element.178), channel_id=1, source_target_pairs={{0,5},{1,6},{2,7},{3,0},{4,1},{5,2},{6,3},{7,4},{8,13},{9,14},{10,... | collective-permute-start | bytes 2312 | tf_op jit(solution)/shard_map/ppermute | solution.py:18
  13.6 7.3 %collective-permute-start.3 = (f32[8,3,2,4]{0,3,2,1:T(4,128)S(1)}, f32[8,3,2,4]{0,3,2,1:T(4,128)S(1)}, u32[]{:S(2)}, u32[]{:S(2)}) collective-permute-start(f32[8,3,2,4]{0,3,2,1:T(4,128)S(1)} %get-tuple-element.177), channel_id=1, source_target_pairs={{0,4},{1,5},{2,6},{3,7},{4,0},{5,1},{6,2},{7,3},{8,12},{9,13},{10,... | collective-permute-start | bytes 2312 | tf_op jit(solution)/shard_map/ppermute | solution.py:18
  16.6 5.5 %collective-permute-start.4 = (f32[8,3,2,4]{0,3,2,1:T(4,128)S(1)}, f32[8,3,2,4]{0,3,2,1:T(4,128)S(1)}, u32[]{:S(2)}, u32[]{:S(2)}) collective-permute-start(f32[8,3,2,4]{0,3,2,1:T(4,128)S(1)} %get-tuple-element.176), channel_id=1, source_target_pairs={{0,3},{1,4},{2,5},{3,6},{4,7},{5,0},{6,1},{7,2},{8,11},{9,12},{10,... | collective-permute-start | bytes 2312 | tf_op jit(solution)/shard_map/ppermute | solution.py:18
  16.7 6.5 %collective-permute-start.5 = (f32[8,3,2,4]{0,3,2,1:T(4,128)S(1)}, f32[8,3,2,4]{0,3,2,1:T(4,128)S(1)}, u32[]{:S(2)}, u32[]{:S(2)}) collective-permute-start(f32[8,3,2,4]{0,3,2,1:T(4,128)S(1)} %get-tuple-element.175), channel_id=1, source_target_pairs={{0,2},{1,3},{2,4},{3,5},{4,6},{5,7},{6,0},{7,1},{8,10},{9,11},{10,... | collective-permute-start | bytes 2312 | tf_op jit(solution)/shard_map/ppermute | solution.py:18
  18.6 6.4 %collective-permute-start.6 = (f32[8,3,2,4]{0,3,2,1:T(4,128)S(1)}, f32[8,3,2,4]{0,3,2,1:T(4,128)S(1)}, u32[]{:S(2)}, u32[]{:S(2)}) collective-permute-start(f32[8,3,2,4]{0,3,2,1:T(4,128)S(1)} %get-tuple-element.174), channel_id=1, source_target_pairs={{0,1},{1,2},{2,3},{3,4},{4,5},{5,6},{6,7},{7,0},{8,9},{9,10},{10,1... | collective-permute-start | bytes 2312 | tf_op jit(solution)/shard_map/ppermute | solution.py:18
